TPU v7x, 128 devices: a whole 4x4x4 slice. The times are simulated.
128 devices in a mesh: blk: 16 (over x, z_lo, core), dp: 8 (over y, z_hi).
Axes of the slice: x: 4, y: 4, z: 4 (z_hi: 2, z_lo: 2; z = z_hi * 2 + z_lo), core: 2. Of those that a mesh axis runs over, the one named last changes fastest.
Arguments:
- x_in: bfloat16 [196608, 896], P(('blk', 'dp')), may hold values from -6 to 6
- cotangent: bfloat16 [98304, 896], P(('blk', 'dp')), may hold values from -0.059814453 to 0.059814453
- seq_len: int32 [16, 8, 8], P('blk'), may hold values from 36 to 204, as said below
- seq_owner: int32 [16, 8, 8], P('blk'), may hold values from 0 to 7, as said below
- proj_master: float32 [2, 896, 2432], P(None, 'dp', 'blk'), may hold values from -0.1875 to 0.1875
- down_master: float32 [2432, 896], P('blk', 'dp'), may hold values from -0.125 to 0.125
- proj_m: float32 [2, 896, 2432], P(None, 'dp', 'blk'), may hold values from -6 to 6
- proj_v: float32 [2, 896, 2432], P(None, 'dp', 'blk'), may hold values from 0.25 to 4
- down_m: float32 [2432, 896], P('blk', 'dp'), may hold values from -6 to 6
- down_v: float32 [2432, 896], P('blk', 'dp'), may hold values from 0.25 to 4
Outputs:
- mixed: bfloat16 [98304, 896], P(('blk', 'dp'))
- new_proj: float32 [2, 896, 2432], P(None, 'dp', 'blk')
- new_down: float32 [2432, 896], P('blk', 'dp')
- new_proj_m: float32 [2, 896, 2432], P(None, 'dp', 'blk')
- new_proj_v: float32 [2, 896, 2432], P(None, 'dp', 'blk')
- new_down_m: float32 [2432, 896], P('blk', 'dp')
- new_down_v: float32 [2432, 896], P('blk', 'dp')
Inputs may be any that keep to these rules, and one draw needn't show every extreme that they name: `seq_len`: row [b, g] lists the token counts of the 8 sequences held by dp index g of blk index b, packed in order from its first row; one device of each blk index fills all 1536 rows; some count equals 204 in every draw; the sequences sent to each dp index of a blk index hold exactly 768 tokens together. Row [b, g] is a permutation of the dp indices: sequence k of dp index g goes to dp index seq_owner[b, g, k] of the same blk index.
All inputs are finite; a program needn't handle non-finite values.
Results may differ from a plain program's by a relative error of at most 0.015.
Values may be sent and summed in bfloat16 or wider, within the bound.
No kernel may reach another device: no remote copies, remote signals or barrier semaphores. Data moves between devices by JAX's collectives and lax.ppermute only.
A program may use at most 128 MiB of HBM per device.

v0:
```python
import jax
import jax.numpy as jnp
from jax import lax
from jax.sharding import PartitionSpec as P

STEP = 100


def passed_along(value, axis, steps):
    count = lax.axis_size(axis)
    pairs = [(source, (source + steps) % count) for source in range(count)]
    return lax.ppermute(value, axis, pairs)


def span_terms(normed, delta, w_proj, w_down):
    gate_val = jnp.dot(normed, w_proj[0], preferred_element_type=jnp.float32)
    up_val = jnp.dot(normed, w_proj[1], preferred_element_type=jnp.float32)
    sigmoid_gate = jax.nn.sigmoid(gate_val)
    silu_gate = gate_val * sigmoid_gate
    hidden = (silu_gate * up_val).astype(jnp.bfloat16)
    branch = jnp.dot(hidden, w_down, preferred_element_type=jnp.float32)
    d_hidden = lax.dot_general(
        delta, w_down, (((1,), (1,)), ((), ())), preferred_element_type=jnp.float32
    )
    d_gate = (d_hidden * up_val * sigmoid_gate * (1.0 + gate_val * (1.0 - sigmoid_gate))).astype(
        jnp.bfloat16
    )
    d_up = (d_hidden * silu_gate).astype(jnp.bfloat16)
    over_rows = (((0,), (0,)), ((), ()))
    grad_down = lax.dot_general(hidden, delta, over_rows, preferred_element_type=jnp.float32)
    grad_gate = lax.dot_general(normed, d_gate, over_rows, preferred_element_type=jnp.float32)
    grad_up = lax.dot_general(normed, d_up, over_rows, preferred_element_type=jnp.float32)
    return (branch, (jnp.stack([grad_gate, grad_up]), grad_down))


def adam(master, grad, first_moment, second_moment):
    first_new = 0.9 * first_moment + 0.1 * grad
    second_new = 0.95 * second_moment + 0.05 * grad * grad
    first_hat = first_new / (1.0 - 0.9**STEP)
    second_hat = second_new / (1.0 - 0.95**STEP)
    updated = master - 0.0003 * (first_hat / (jnp.sqrt(second_hat) + 1e-08) + 0.1 * master)
    return (updated, first_new, second_new)


def rebalance(x_in, seq_len, seq_owner, out_cap):
    dp_count = lax.axis_size("dp")
    own_index = lax.axis_index("dp")
    counts_all = seq_len[0]
    owners_all = seq_owner[0]
    dev_ids = jnp.arange(dp_count, dtype=jnp.int32)
    owner_hot = (owners_all[:, :, None] == dev_ids[None, None, :]).astype(jnp.int32)
    starts = jnp.cumsum(counts_all, axis=1) - counts_all
    len_to = jnp.sum(counts_all[:, :, None] * owner_hot, axis=1)
    start_to = jnp.sum(starts[:, :, None] * owner_hot, axis=1)
    pair_size = out_cap // dp_count
    slot_size = 2 * pair_size + pair_size // 8
    own_len = lax.dynamic_index_in_dim(len_to, own_index, 0, keepdims=False)
    own_start = lax.dynamic_index_in_dim(start_to, own_index, 0, keepdims=False)
    slot_ids = jnp.arange(slot_size, dtype=jnp.int32)
    source_row = jnp.minimum(own_start[:, None] + slot_ids[None, :], x_in.shape[0] - 1)
    valid = slot_ids[None, :] < own_len[:, None]
    packed = jnp.take(x_in, source_row.reshape(-1), axis=0)
    packed = jnp.where(valid.reshape(-1, 1), packed, jnp.zeros((), jnp.bfloat16))
    arrived = lax.all_to_all(packed, "dp", split_axis=0, concat_axis=0, tiled=True)
    incoming = lax.dynamic_index_in_dim(len_to, own_index, 1, keepdims=False)
    offsets = jnp.cumsum(incoming) - incoming
    row_ids = jnp.arange(out_cap, dtype=jnp.int32)
    source_dev = jnp.sum((row_ids[:, None] >= offsets[None, :]).astype(jnp.int32), axis=1) - 1
    pick = (source_dev[:, None] == dev_ids[None, :]).astype(jnp.int32)
    base = jnp.sum(pick * offsets[None, :], axis=1)
    return jnp.take(arrived, source_dev * slot_size + row_ids - base, axis=0)


def per_device(
    x_in, cotangent, seq_len, seq_owner, proj_master, down_master, proj_m, proj_v, down_m, down_v
):
    out_cap = cotangent.shape[0]
    tokens = rebalance(x_in, seq_len, seq_owner, out_cap)
    widened = tokens.astype(jnp.float32)
    scale = lax.rsqrt(jnp.mean(widened * widened, axis=1, keepdims=True) + 1e-06)
    normed = (widened * scale).astype(jnp.bfloat16)
    w_proj, w_down = (
        lax.all_gather(proj_master.astype(jnp.bfloat16), "dp", axis=1, tiled=True),
        lax.all_gather(down_master.astype(jnp.bfloat16), "dp", axis=1, tiled=True),
    )
    blk_count = lax.axis_size("blk")
    own_block = lax.axis_index("blk")
    proj_shape, down_shape = (w_proj.shape, w_down.shape)
    store_proj = jnp.zeros((blk_count,) + proj_shape, jnp.float32)
    store_down = jnp.zeros((blk_count,) + down_shape, jnp.float32)

    def keep_terms(turn_index, held_proj, held_down, running, kept_proj, kept_down):
        branch, grads = span_terms(normed, cotangent, held_proj, held_down)
        grad_proj, grad_down = grads
        position = (own_block - turn_index) % blk_count
        kept_proj = lax.dynamic_update_index_in_dim(kept_proj, grad_proj, position, 0)
        kept_down = lax.dynamic_update_index_in_dim(kept_down, grad_down, position, 0)
        return (running + branch, kept_proj, kept_down)

    def forward(turn_index, state_tuple):
        held_proj, held_down, running, kept_proj, kept_down = state_tuple
        running, kept_proj, kept_down = keep_terms(
            turn_index, held_proj, held_down, running, kept_proj, kept_down
        )
        held_proj, held_down = passed_along((held_proj, held_down), "blk", 1)
        return (held_proj, held_down, running, kept_proj, kept_down)

    held_proj, held_down, running, kept_proj, kept_down = lax.fori_loop(
        0, blk_count - 1, forward, (w_proj, w_down, widened, store_proj, store_down)
    )
    running, kept_proj, kept_down = keep_terms(
        blk_count - 1, held_proj, held_down, running, kept_proj, kept_down
    )

    def backward(turn_index, sums):
        acc_proj, acc_down = (
            passed_along(sums[0].astype(jnp.bfloat16), "blk", -1).astype(jnp.float32),
            passed_along(sums[1].astype(jnp.bfloat16), "blk", -1).astype(jnp.float32),
        )
        position = (own_block + turn_index + 1) % blk_count
        acc_proj = acc_proj + lax.dynamic_index_in_dim(kept_proj, position, 0, keepdims=False)
        acc_down = acc_down + lax.dynamic_index_in_dim(kept_down, position, 0, keepdims=False)
        return (acc_proj, acc_down)

    first_pos = (own_block + 1) % blk_count
    first_sums = (
        lax.dynamic_index_in_dim(kept_proj, first_pos, 0, keepdims=False),
        lax.dynamic_index_in_dim(kept_down, first_pos, 0, keepdims=False),
    )
    acc_proj, acc_down = lax.fori_loop(1, blk_count, backward, first_sums)
    acc_proj, acc_down = (
        lax.psum_scatter(
            acc_proj.astype(jnp.bfloat16), "dp", scatter_dimension=1, tiled=True
        ).astype(jnp.float32),
        lax.psum_scatter(
            acc_down.astype(jnp.bfloat16), "dp", scatter_dimension=1, tiled=True
        ).astype(jnp.float32),
    )
    mixed = running.astype(jnp.bfloat16)
    new_proj, new_proj_m, new_proj_v = adam(proj_master, acc_proj, proj_m, proj_v)
    new_down, new_down_m, new_down_v = adam(down_master, acc_down, down_m, down_v)
    return (mixed, new_proj, new_down, new_proj_m, new_proj_v, new_down_m, new_down_v)


def solution(mesh):
    in_specs = (
        P(("blk", "dp"), None),
        P(("blk", "dp"), None),
        P("blk", None, None),
        P("blk", None, None),
        P(None, "dp", "blk"),
        P("blk", "dp"),
        P(None, "dp", "blk"),
        P(None, "dp", "blk"),
        P("blk", "dp"),
        P("blk", "dp"),
    )
    out_specs = (
        P(("blk", "dp"), None),
        P(None, "dp", "blk"),
        P("blk", "dp"),
        P(None, "dp", "blk"),
        P(None, "dp", "blk"),
        P("blk", "dp"),
        P("blk", "dp"),
    )
    return jax.shard_map(
        per_device, mesh=mesh, in_specs=in_specs, out_specs=out_specs, check_vma=False
    )
```

profile of v0, /device:TPU:0, one launch (start us, length us, event | category | flops | bytes accessed | tf_op | source)
XLA Modules:
  0.0 880.4 jit_solution(11480174296041936787)
XLA Ops:
  10.0 6.4 gather_fusion
  16.4 4.3 gather.11
  24.2 8.0 all-to-all-start
  32.6 73.6 %all_gather.6 = bf16[2,896,152]{2,0,1:T(2,128)(2,1)} all-gather(bf16[2,112,152]{2,0,1:T(2,128)(2,1)S(1)} %copy.34), channel_id=1, replica_groups=mesh['blk'=16,'dp'=8] {'dp'}, dimensions={1}, use_global_device_ids=true | all-gather | bytes 612864 | tf_op jit(solution)/shard_map/all_gather | solution.py:83
  109.7 34.7 %all-gather = bf16[8,112,152]{1,2,0:T(8,128)(2,1)S(1)} all-gather(bf16[1,112,152]{1,2,0:T(8,128)(2,1)S(1)} %convert_bitcast_fusion), channel_id=1, replica_groups=mesh['blk'=16,'dp'=8] {'dp'}, dimensions={0}, use_global_device_ids=true | all-gather | bytes 306432 | tf_op jit(solution)/shard_map/all_gather | solution.py:84
  145.2 4.3 all_to_all.7
  149.5 6.4 gather_fusion.1
  161.2 7.2 broadcast_in_dim.84
  172.3 272.5 %while.40 = (s32[]{:T(128)}, bf16[2,896,152]{1,2,0:T(8,128)(2,1)}, bf16[152,896]{1,0:T(8,128)(2,1)S(1)}, f32[768,896]{1,0:T(8,128)}, f32[16,2,896,152]{2,3,1,0:T...) while((s32[]{:T(128)}, bf16[2,896,152]{1,2,0:T(8,128)(2,1)}, ...), condition=%wide.region_8.9_spmd, body=%wide.region_7.8_spmd.sunk | while | flops 1467865088 | bytes 44986812 | solution.py:108
  185.0 4.0 convolution_add_fusion.2
  221.6 4.0 convolution_add_fusion.2
  312.2 4.0 convolution_add_fusion.2
  403.3 4.0 convolution_add_fusion.2
  439.6 4.0 convolution_add_fusion.2
  456.6 271.4 %while.41 = (s32[]{:T(128)}, bf16[2,896,152]{1,2,0:T(8,128)(2,1)}, bf16[152,896]{1,0:T(8,128)(2,1)}, s32[]{:T(128)}, f32[16,2,896,152]{2,3,1,0:T(8,128)}, /*inde...) while((s32[]{:T(128)}, bf16[2,896,152]{1,2,0:T(8,128)(2,1)}, ...), condition=%wide.region_10.11_spmd, body=%wide.region_9.10_spmd.sunk | while | flops 1225746 | bytes 6537572 | solution.py:130
  459.8 9.7 %collective-permute-done.3 = bf16[152,896]{1,0:T(8,128)(2,1)S(1)} collective-permute-done((bf16[152,896]{1,0:T(8,128)(2,1)}, bf16[152,896]{1,0:T(8,128)(2,1)S(1)}, u32[]{:S(2)}, u32[]{:S(2)}) %collective-permute-start.3) | collective-permute-done | bytes 272416 | tf_op jit(solution)/shard_map/while/body/eval_jaxpr/ppermute | solution.py:12
  477.6 10.1 %collective-permute-done.3 = bf16[152,896]{1,0:T(8,128)(2,1)S(1)} collective-permute-done((bf16[152,896]{1,0:T(8,128)(2,1)}, bf16[152,896]{1,0:T(8,128)(2,1)S(1)}, u32[]{:S(2)}, u32[]{:S(2)}) %collective-permute-start.3) | collective-permute-done | bytes 272416 | tf_op jit(solution)/shard_map/while/body/eval_jaxpr/ppermute | solution.py:12
  495.7 10.1 %collective-permute-done.3 = bf16[152,896]{1,0:T(8,128)(2,1)S(1)} collective-permute-done((bf16[152,896]{1,0:T(8,128)(2,1)}, bf16[152,896]{1,0:T(8,128)(2,1)S(1)}, u32[]{:S(2)}, u32[]{:S(2)}) %collective-permute-start.3) | collective-permute-done | bytes 272416 | tf_op jit(solution)/shard_map/while/body/eval_jaxpr/ppermute | solution.py:12
  513.9 10.1 %collective-permute-done.3 = bf16[152,896]{1,0:T(8,128)(2,1)S(1)} collective-permute-done((bf16[152,896]{1,0:T(8,128)(2,1)}, bf16[152,896]{1,0:T(8,128)(2,1)S(1)}, u32[]{:S(2)}, u32[]{:S(2)}) %collective-permute-start.3) | collective-permute-done | bytes 272416 | tf_op jit(solution)/shard_map/while/body/eval_jaxpr/ppermute | solution.py:12
  532.1 10.1 %collective-permute-done.3 = bf16[152,896]{1,0:T(8,128)(2,1)S(1)} collective-permute-done((bf16[152,896]{1,0:T(8,128)(2,1)}, bf16[152,896]{1,0:T(8,128)(2,1)S(1)}, u32[]{:S(2)}, u32[]{:S(2)}) %collective-permute-start.3) | collective-permute-done | bytes 272416 | tf_op jit(solution)/shard_map/while/body/eval_jaxpr/ppermute | solution.py:12
  550.3 10.1 %collective-permute-done.3 = bf16[152,896]{1,0:T(8,128)(2,1)S(1)} collective-permute-done((bf16[152,896]{1,0:T(8,128)(2,1)}, bf16[152,896]{1,0:T(8,128)(2,1)S(1)}, u32[]{:S(2)}, u32[]{:S(2)}) %collective-permute-start.3) | collective-permute-done | bytes 272416 | tf_op jit(solution)/shard_map/while/body/eval_jaxpr/ppermute | solution.py:12
  568.4 10.1 %collective-permute-done.3 = bf16[152,896]{1,0:T(8,128)(2,1)S(1)} collective-permute-done((bf16[152,896]{1,0:T(8,128)(2,1)}, bf16[152,896]{1,0:T(8,128)(2,1)S(1)}, u32[]{:S(2)}, u32[]{:S(2)}) %collective-permute-start.3) | collective-permute-done | bytes 272416 | tf_op jit(solution)/shard_map/while/body/eval_jaxpr/ppermute | solution.py:12
  586.6 10.1 %collective-permute-done.3 = bf16[152,896]{1,0:T(8,128)(2,1)S(1)} collective-permute-done((bf16[152,896]{1,0:T(8,128)(2,1)}, bf16[152,896]{1,0:T(8,128)(2,1)S(1)}, u32[]{:S(2)}, u32[]{:S(2)}) %collective-permute-start.3) | collective-permute-done | bytes 272416 | tf_op jit(solution)/shard_map/while/body/eval_jaxpr/ppermute | solution.py:12
  604.8 10.1 %collective-permute-done.3 = bf16[152,896]{1,0:T(8,128)(2,1)S(1)} collective-permute-done((bf16[152,896]{1,0:T(8,128)(2,1)}, bf16[152,896]{1,0:T(8,128)(2,1)S(1)}, u32[]{:S(2)}, u32[]{:S(2)}) %collective-permute-start.3) | collective-permute-done | bytes 272416 | tf_op jit(solution)/shard_map/while/body/eval_jaxpr/ppermute | solution.py:12
  622.9 10.1 %collective-permute-done.3 = bf16[152,896]{1,0:T(8,128)(2,1)S(1)} collective-permute-done((bf16[152,896]{1,0:T(8,128)(2,1)}, bf16[152,896]{1,0:T(8,128)(2,1)S(1)}, u32[]{:S(2)}, u32[]{:S(2)}) %collective-permute-start.3) | collective-permute-done | bytes 272416 | tf_op jit(solution)/shard_map/while/body/eval_jaxpr/ppermute | solution.py:12
  641.1 10.1 %collective-permute-done.3 = bf16[152,896]{1,0:T(8,128)(2,1)S(1)} collective-permute-done((bf16[152,896]{1,0:T(8,128)(2,1)}, bf16[152,896]{1,0:T(8,128)(2,1)S(1)}, u32[]{:S(2)}, u32[]{:S(2)}) %collective-permute-start.3) | collective-permute-done | bytes 272416 | tf_op jit(solution)/shard_map/while/body/eval_jaxpr/ppermute | solution.py:12
  659.3 10.1 %collective-permute-done.3 = bf16[152,896]{1,0:T(8,128)(2,1)S(1)} collective-permute-done((bf16[152,896]{1,0:T(8,128)(2,1)}, bf16[152,896]{1,0:T(8,128)(2,1)S(1)}, u32[]{:S(2)}, u32[]{:S(2)}) %collective-permute-start.3) | collective-permute-done | bytes 272416 | tf_op jit(solution)/shard_map/while/body/eval_jaxpr/ppermute | solution.py:12
  677.5 10.1 %collective-permute-done.3 = bf16[152,896]{1,0:T(8,128)(2,1)S(1)} collective-permute-done((bf16[152,896]{1,0:T(8,128)(2,1)}, bf16[152,896]{1,0:T(8,128)(2,1)S(1)}, u32[]{:S(2)}, u32[]{:S(2)}) %collective-permute-start.3) | collective-permute-done | bytes 272416 | tf_op jit(solution)/shard_map/while/body/eval_jaxpr/ppermute | solution.py:12
  695.6 10.1 %collective-permute-done.3 = bf16[152,896]{1,0:T(8,128)(2,1)S(1)} collective-permute-done((bf16[152,896]{1,0:T(8,128)(2,1)}, bf16[152,896]{1,0:T(8,128)(2,1)S(1)}, u32[]{:S(2)}, u32[]{:S(2)}) %collective-permute-start.3) | collective-permute-done | bytes 272416 | tf_op jit(solution)/shard_map/while/body/eval_jaxpr/ppermute | solution.py:12
  713.8 10.1 %collective-permute-done.3 = bf16[152,896]{1,0:T(8,128)(2,1)S(1)} collective-permute-done((bf16[152,896]{1,0:T(8,128)(2,1)}, bf16[152,896]{1,0:T(8,128)(2,1)S(1)}, u32[]{:S(2)}, u32[]{:S(2)}) %collective-permute-start.3) | collective-permute-done | bytes 272416 | tf_op jit(solution)/shard_map/while/body/eval_jaxpr/ppermute | solution.py:12
  740.8 57.8 %reduce-scatter.9.cloned.1.call-done = bf16[112,152]{1,0:T(8,128)(2,1)} async-done(((bf16[896,152]{1,0:T(8,128)(2,1)}), bf16[112,152]{1,0:T(8,128)(2,1)}) %reduce-scatter.9.cloned.1.call-update) | async-done | bytes 34064
  801.1 69.4 %reduce-scatter.7.cloned.1.call-done = bf16[112,304]{1,0:T(8,128)(2,1)} async-done(((bf16[896,304]{1,0:T(8,128)(2,1)}), bf16[112,304]{1,0:T(8,128)(2,1)}) %reduce-scatter.7.cloned.1.call-update) | async-done | bytes 68112
  (440 shorter events, 421.8 us)
Async XLA Ops:
  24.2 120.9 %all-to-all-start = ((bf16[8,204,896]{2,1,0:T(8,128)(2,1)}), bf16[8,204,896]{2,1,0:T(8,128)(2,1)}, u32[]{:S(2)}, u32[]{:S(2)}) async-start(bf16[8,204,896]{2,1,0:T(8,128)(2,1)} %select_select_fusion), calls=%async_computation | async-start | bytes 5963776 | tf_op jit(solution)/shard_map/all_to_all | solution.py:64
  32.2 766.3 %reduce-scatter.9.cloned.1.call-start = ((), (), s32[]{:S(2)}) async-start(), calls=%async_computation.4 | async-start | bytes 516096
  174.2 16.0 %collective-permute-start = (bf16[2,896,152]{1,2,0:T(8,128)(2,1)}, bf16[2,896,152]{1,2,0:T(8,128)(2,1)}, u32[]{:S(2)}, u32[]{:S(2)}) collective-permute-start(bf16[2,896,152]{1,2,0:T(8,128)(2,1)} %copy.50), channel_id=1, source_target_pairs={{0,8},{8,16},{16,24},{24,32},{32,40},{40,48},{48,56},{56,64},{64,7... | collective-permute-start | bytes 1634312 | tf_op jit(solution)/shard_map/while/body/eval_jaxpr/ppermute | solution.py:12
  174.3 16.0 %collective-permute-start.1 = (bf16[152,896]{1,0:T(8,128)(2,1)S(1)}, bf16[152,896]{1,0:T(8,128)(2,1)S(1)}, u32[]{:S(2)}, u32[]{:S(2)}) collective-permute-start(bf16[152,896]{1,0:T(8,128)(2,1)S(1)} %copy.51), channel_id=1, source_target_pairs={{0,8},{8,16},{16,24},{24,32},{32,40},{40,48},{48,56},{56,64},{64,7... | collective-permute-start | bytes 817160 | tf_op jit(solution)/shard_map/while/body/eval_jaxpr/ppermute | solution.py:12
  192.2 16.7 %collective-permute-start = (bf16[2,896,152]{1,2,0:T(8,128)(2,1)}, bf16[2,896,152]{1,2,0:T(8,128)(2,1)}, u32[]{:S(2)}, u32[]{:S(2)}) collective-permute-start(bf16[2,896,152]{1,2,0:T(8,128)(2,1)} %copy.50), channel_id=1, source_target_pairs={{0,8},{8,16},{16,24},{24,32},{32,40},{40,48},{48,56},{56,64},{64,7... | collective-permute-start | bytes 1634312 | tf_op jit(solution)/shard_map/while/body/eval_jaxpr/ppermute | solution.py:12
  192.3 16.6 %collective-permute-start.1 = (bf16[152,896]{1,0:T(8,128)(2,1)S(1)}, bf16[152,896]{1,0:T(8,128)(2,1)S(1)}, u32[]{:S(2)}, u32[]{:S(2)}) collective-permute-start(bf16[152,896]{1,0:T(8,128)(2,1)S(1)} %copy.51), channel_id=1, source_target_pairs={{0,8},{8,16},{16,24},{24,32},{32,40},{40,48},{48,56},{56,64},{64,7... | collective-permute-start | bytes 817160 | tf_op jit(solution)/shard_map/while/body/eval_jaxpr/ppermute | solution.py:12
  210.8 16.1 %collective-permute-start = (bf16[2,896,152]{1,2,0:T(8,128)(2,1)}, bf16[2,896,152]{1,2,0:T(8,128)(2,1)}, u32[]{:S(2)}, u32[]{:S(2)}) collective-permute-start(bf16[2,896,152]{1,2,0:T(8,128)(2,1)} %copy.50), channel_id=1, source_target_pairs={{0,8},{8,16},{16,24},{24,32},{32,40},{40,48},{48,56},{56,64},{64,7... | collective-permute-start | bytes 1634312 | tf_op jit(solution)/shard_map/while/body/eval_jaxpr/ppermute | solution.py:12
  210.9 16.1 %collective-permute-start.1 = (bf16[152,896]{1,0:T(8,128)(2,1)S(1)}, bf16[152,896]{1,0:T(8,128)(2,1)S(1)}, u32[]{:S(2)}, u32[]{:S(2)}) collective-permute-start(bf16[152,896]{1,0:T(8,128)(2,1)S(1)} %copy.51), channel_id=1, source_target_pairs={{0,8},{8,16},{16,24},{24,32},{32,40},{40,48},{48,56},{56,64},{64,7... | collective-permute-start | bytes 817160 | tf_op jit(solution)/shard_map/while/body/eval_jaxpr/ppermute | solution.py:12
  228.9 16.5 %collective-permute-start = (bf16[2,896,152]{1,2,0:T(8,128)(2,1)}, bf16[2,896,152]{1,2,0:T(8,128)(2,1)}, u32[]{:S(2)}, u32[]{:S(2)}) collective-permute-start(bf16[2,896,152]{1,2,0:T(8,128)(2,1)} %copy.50), channel_id=1, source_target_pairs={{0,8},{8,16},{16,24},{24,32},{32,40},{40,48},{48,56},{56,64},{64,7... | collective-permute-start | bytes 1634312 | tf_op jit(solution)/shard_map/while/body/eval_jaxpr/ppermute | solution.py:12
  228.9 16.5 %collective-permute-start.1 = (bf16[152,896]{1,0:T(8,128)(2,1)S(1)}, bf16[152,896]{1,0:T(8,128)(2,1)S(1)}, u32[]{:S(2)}, u32[]{:S(2)}) collective-permute-start(bf16[152,896]{1,0:T(8,128)(2,1)S(1)} %copy.51), channel_id=1, source_target_pairs={{0,8},{8,16},{16,24},{24,32},{32,40},{40,48},{48,56},{56,64},{64,7... | collective-permute-start | bytes 817160 | tf_op jit(solution)/shard_map/while/body/eval_jaxpr/ppermute | solution.py:12
  247.3 16.3 %collective-permute-start = (bf16[2,896,152]{1,2,0:T(8,128)(2,1)}, bf16[2,896,152]{1,2,0:T(8,128)(2,1)}, u32[]{:S(2)}, u32[]{:S(2)}) collective-permute-start(bf16[2,896,152]{1,2,0:T(8,128)(2,1)} %copy.50), channel_id=1, source_target_pairs={{0,8},{8,16},{16,24},{24,32},{32,40},{40,48},{48,56},{56,64},{64,7... | collective-permute-start | bytes 1634312 | tf_op jit(solution)/shard_map/while/body/eval_jaxpr/ppermute | solution.py:12
  247.6 16.0 %collective-permute-start.1 = (bf16[152,896]{1,0:T(8,128)(2,1)S(1)}, bf16[152,896]{1,0:T(8,128)(2,1)S(1)}, u32[]{:S(2)}, u32[]{:S(2)}) collective-permute-start(bf16[152,896]{1,0:T(8,128)(2,1)S(1)} %copy.51), channel_id=1, source_target_pairs={{0,8},{8,16},{16,24},{24,32},{32,40},{40,48},{48,56},{56,64},{64,7... | collective-permute-start | bytes 817160 | tf_op jit(solution)/shard_map/while/body/eval_jaxpr/ppermute | solution.py:12
  265.5 16.4 %collective-permute-start = (bf16[2,896,152]{1,2,0:T(8,128)(2,1)}, bf16[2,896,152]{1,2,0:T(8,128)(2,1)}, u32[]{:S(2)}, u32[]{:S(2)}) collective-permute-start(bf16[2,896,152]{1,2,0:T(8,128)(2,1)} %copy.50), channel_id=1, source_target_pairs={{0,8},{8,16},{16,24},{24,32},{32,40},{40,48},{48,56},{56,64},{64,7... | collective-permute-start | bytes 1634312 | tf_op jit(solution)/shard_map/while/body/eval_jaxpr/ppermute | solution.py:12
  265.5 16.4 %collective-permute-start.1 = (bf16[152,896]{1,0:T(8,128)(2,1)S(1)}, bf16[152,896]{1,0:T(8,128)(2,1)S(1)}, u32[]{:S(2)}, u32[]{:S(2)}) collective-permute-start(bf16[152,896]{1,0:T(8,128)(2,1)S(1)} %copy.51), channel_id=1, source_target_pairs={{0,8},{8,16},{16,24},{24,32},{32,40},{40,48},{48,56},{56,64},{64,7... | collective-permute-start | bytes 817160 | tf_op jit(solution)/shard_map/while/body/eval_jaxpr/ppermute | solution.py:12
  283.8 15.9 %collective-permute-start = (bf16[2,896,152]{1,2,0:T(8,128)(2,1)}, bf16[2,896,152]{1,2,0:T(8,128)(2,1)}, u32[]{:S(2)}, u32[]{:S(2)}) collective-permute-start(bf16[2,896,152]{1,2,0:T(8,128)(2,1)} %copy.50), channel_id=1, source_target_pairs={{0,8},{8,16},{16,24},{24,32},{32,40},{40,48},{48,56},{56,64},{64,7... | collective-permute-start | bytes 1634312 | tf_op jit(solution)/shard_map/while/body/eval_jaxpr/ppermute | solution.py:12
  301.6 15.9 %collective-permute-start = (bf16[2,896,152]{1,2,0:T(8,128)(2,1)}, bf16[2,896,152]{1,2,0:T(8,128)(2,1)}, u32[]{:S(2)}, u32[]{:S(2)}) collective-permute-start(bf16[2,896,152]{1,2,0:T(8,128)(2,1)} %copy.50), channel_id=1, source_target_pairs={{0,8},{8,16},{16,24},{24,32},{32,40},{40,48},{48,56},{56,64},{64,7... | collective-permute-start | bytes 1634312 | tf_op jit(solution)/shard_map/while/body/eval_jaxpr/ppermute | solution.py:12
  319.4 16.0 %collective-permute-start = (bf16[2,896,152]{1,2,0:T(8,128)(2,1)}, bf16[2,896,152]{1,2,0:T(8,128)(2,1)}, u32[]{:S(2)}, u32[]{:S(2)}) collective-permute-start(bf16[2,896,152]{1,2,0:T(8,128)(2,1)} %copy.50), channel_id=1, source_target_pairs={{0,8},{8,16},{16,24},{24,32},{32,40},{40,48},{48,56},{56,64},{64,7... | collective-permute-start | bytes 1634312 | tf_op jit(solution)/shard_map/while/body/eval_jaxpr/ppermute | solution.py:12
  319.5 16.0 %collective-permute-start.1 = (bf16[152,896]{1,0:T(8,128)(2,1)S(1)}, bf16[152,896]{1,0:T(8,128)(2,1)S(1)}, u32[]{:S(2)}, u32[]{:S(2)}) collective-permute-start(bf16[152,896]{1,0:T(8,128)(2,1)S(1)} %copy.51), channel_id=1, source_target_pairs={{0,8},{8,16},{16,24},{24,32},{32,40},{40,48},{48,56},{56,64},{64,7... | collective-permute-start | bytes 817160 | tf_op jit(solution)/shard_map/while/body/eval_jaxpr/ppermute | solution.py:12
  337.3 16.6 %collective-permute-start = (bf16[2,896,152]{1,2,0:T(8,128)(2,1)}, bf16[2,896,152]{1,2,0:T(8,128)(2,1)}, u32[]{:S(2)}, u32[]{:S(2)}) collective-permute-start(bf16[2,896,152]{1,2,0:T(8,128)(2,1)} %copy.50), channel_id=1, source_target_pairs={{0,8},{8,16},{16,24},{24,32},{32,40},{40,48},{48,56},{56,64},{64,7... | collective-permute-start | bytes 1634312 | tf_op jit(solution)/shard_map/while/body/eval_jaxpr/ppermute | solution.py:12
  337.5 16.4 %collective-permute-start.1 = (bf16[152,896]{1,0:T(8,128)(2,1)S(1)}, bf16[152,896]{1,0:T(8,128)(2,1)S(1)}, u32[]{:S(2)}, u32[]{:S(2)}) collective-permute-start(bf16[152,896]{1,0:T(8,128)(2,1)S(1)} %copy.51), channel_id=1, source_target_pairs={{0,8},{8,16},{16,24},{24,32},{32,40},{40,48},{48,56},{56,64},{64,7... | collective-permute-start | bytes 817160 | tf_op jit(solution)/shard_map/while/body/eval_jaxpr/ppermute | solution.py:12
  355.8 16.3 %collective-permute-start = (bf16[2,896,152]{1,2,0:T(8,128)(2,1)}, bf16[2,896,152]{1,2,0:T(8,128)(2,1)}, u32[]{:S(2)}, u32[]{:S(2)}) collective-permute-start(bf16[2,896,152]{1,2,0:T(8,128)(2,1)} %copy.50), channel_id=1, source_target_pairs={{0,8},{8,16},{16,24},{24,32},{32,40},{40,48},{48,56},{56,64},{64,7... | collective-permute-start | bytes 1634312 | tf_op jit(solution)/shard_map/while/body/eval_jaxpr/ppermute | solution.py:12
  356.1 16.0 %collective-permute-start.1 = (bf16[152,896]{1,0:T(8,128)(2,1)S(1)}, bf16[152,896]{1,0:T(8,128)(2,1)S(1)}, u32[]{:S(2)}, u32[]{:S(2)}) collective-permute-start(bf16[152,896]{1,0:T(8,128)(2,1)S(1)} %copy.51), channel_id=1, source_target_pairs={{0,8},{8,16},{16,24},{24,32},{32,40},{40,48},{48,56},{56,64},{64,7... | collective-permute-start | bytes 817160 | tf_op jit(solution)/shard_map/while/body/eval_jaxpr/ppermute | solution.py:12
  374.0 16.6 %collective-permute-start = (bf16[2,896,152]{1,2,0:T(8,128)(2,1)}, bf16[2,896,152]{1,2,0:T(8,128)(2,1)}, u32[]{:S(2)}, u32[]{:S(2)}) collective-permute-start(bf16[2,896,152]{1,2,0:T(8,128)(2,1)} %copy.50), channel_id=1, source_target_pairs={{0,8},{8,16},{16,24},{24,32},{32,40},{40,48},{48,56},{56,64},{64,7... | collective-permute-start | bytes 1634312 | tf_op jit(solution)/shard_map/while/body/eval_jaxpr/ppermute | solution.py:12
  374.1 16.5 %collective-permute-start.1 = (bf16[152,896]{1,0:T(8,128)(2,1)S(1)}, bf16[152,896]{1,0:T(8,128)(2,1)S(1)}, u32[]{:S(2)}, u32[]{:S(2)}) collective-permute-start(bf16[152,896]{1,0:T(8,128)(2,1)S(1)} %copy.51), channel_id=1, source_target_pairs={{0,8},{8,16},{16,24},{24,32},{32,40},{40,48},{48,56},{56,64},{64,7... | collective-permute-start | bytes 817160 | tf_op jit(solution)/shard_map/while/body/eval_jaxpr/ppermute | solution.py:12
  392.5 16.1 %collective-permute-start = (bf16[2,896,152]{1,2,0:T(8,128)(2,1)}, bf16[2,896,152]{1,2,0:T(8,128)(2,1)}, u32[]{:S(2)}, u32[]{:S(2)}) collective-permute-start(bf16[2,896,152]{1,2,0:T(8,128)(2,1)} %copy.50), channel_id=1, source_target_pairs={{0,8},{8,16},{16,24},{24,32},{32,40},{40,48},{48,56},{56,64},{64,7... | collective-permute-start | bytes 1634312 | tf_op jit(solution)/shard_map/while/body/eval_jaxpr/ppermute | solution.py:12
  410.4 16.6 %collective-permute-start = (bf16[2,896,152]{1,2,0:T(8,128)(2,1)}, bf16[2,896,152]{1,2,0:T(8,128)(2,1)}, u32[]{:S(2)}, u32[]{:S(2)}) collective-permute-start(bf16[2,896,152]{1,2,0:T(8,128)(2,1)} %copy.50), channel_id=1, source_target_pairs={{0,8},{8,16},{16,24},{24,32},{32,40},{40,48},{48,56},{56,64},{64,7... | collective-permute-start | bytes 1634312 | tf_op jit(solution)/shard_map/while/body/eval_jaxpr/ppermute | solution.py:12
  410.8 16.2 %collective-permute-start.1 = (bf16[152,896]{1,0:T(8,128)(2,1)S(1)}, bf16[152,896]{1,0:T(8,128)(2,1)S(1)}, u32[]{:S(2)}, u32[]{:S(2)}) collective-permute-start(bf16[152,896]{1,0:T(8,128)(2,1)S(1)} %copy.51), channel_id=1, source_target_pairs={{0,8},{8,16},{16,24},{24,32},{32,40},{40,48},{48,56},{56,64},{64,7... | collective-permute-start | bytes 817160 | tf_op jit(solution)/shard_map/while/body/eval_jaxpr/ppermute | solution.py:12
  428.9 16.0 %collective-permute-start = (bf16[2,896,152]{1,2,0:T(8,128)(2,1)}, bf16[2,896,152]{1,2,0:T(8,128)(2,1)}, u32[]{:S(2)}, u32[]{:S(2)}) collective-permute-start(bf16[2,896,152]{1,2,0:T(8,128)(2,1)} %copy.50), channel_id=1, source_target_pairs={{0,8},{8,16},{16,24},{24,32},{32,40},{40,48},{48,56},{56,64},{64,7... | collective-permute-start | bytes 1634312 | tf_op jit(solution)/shard_map/while/body/eval_jaxpr/ppermute | solution.py:12
  429.0 15.9 %collective-permute-start.1 = (bf16[152,896]{1,0:T(8,128)(2,1)S(1)}, bf16[152,896]{1,0:T(8,128)(2,1)S(1)}, u32[]{:S(2)}, u32[]{:S(2)}) collective-permute-start(bf16[152,896]{1,0:T(8,128)(2,1)S(1)} %copy.51), channel_id=1, source_target_pairs={{0,8},{8,16},{16,24},{24,32},{32,40},{40,48},{48,56},{56,64},{64,7... | collective-permute-start | bytes 817160 | tf_op jit(solution)/shard_map/while/body/eval_jaxpr/ppermute | solution.py:12
  528.1 15.9 %collective-permute-start.2 = (bf16[2,896,152]{1,2,0:T(8,128)(2,1)}, bf16[2,896,152]{1,2,0:T(8,128)(2,1)}, u32[]{:S(2)}, u32[]{:S(2)}) collective-permute-start(bf16[2,896,152]{1,2,0:T(8,128)(2,1)} %get-tuple-element.614), channel_id=1, source_target_pairs={{0,120},{8,0},{16,8},{24,16},{32,24},{40,32},{48,40},{56,48},{64,5... | collective-permute-start | bytes 1634312 | tf_op jit(solution)/shard_map/while/body/eval_jaxpr/ppermute | solution.py:12
  582.7 15.9 %collective-permute-start.2 = (bf16[2,896,152]{1,2,0:T(8,128)(2,1)}, bf16[2,896,152]{1,2,0:T(8,128)(2,1)}, u32[]{:S(2)}, u32[]{:S(2)}) collective-permute-start(bf16[2,896,152]{1,2,0:T(8,128)(2,1)} %get-tuple-element.614), channel_id=1, source_target_pairs={{0,120},{8,0},{16,8},{24,16},{32,24},{40,32},{48,40},{56,48},{64,5... | collective-permute-start | bytes 1634312 | tf_op jit(solution)/shard_map/while/body/eval_jaxpr/ppermute | solution.py:12
  730.0 140.6 %reduce-scatter.7.cloned.1.call-start = ((), (), s32[]{:S(2)}) async-start(), calls=%async_computation.3 | async-start | bytes 774144
  (84 other events, 814.0 us)
Sparse Core Ops, SparseCore 0:
  730.1 68.4 reduce-scatter.8
  802.6 67.8 reduce-scatter.6
where the time goes:
time: 884 us; the launch traced here: 880 us
  waiting for transfers between devices  279 us (32%)
  matrix products  195 us (22%)
  other arithmetic  112 us (13%)
  blocking collectives  108 us (12%)
  starting transfers between devices  89.7 us (10%)
  local copies, waits for them, and re-layouts  80.7 us (9%)
  between operations  14.3 us (2%)
    ppermute x60, waiting for transfers between devices, passed_along(): return lax.ppermute(value, axis, pairs)  152 us
    unnamed x4, waiting for transfers between devices  127 us
    ppermute x60, starting transfers between devices, passed_along(): return lax.ppermute(value, axis, pairs)  81.4 us
    all_gather x1, blocking collectives, per_device(): lax.all_gather(proj_master.astype(jnp.bfloat16), 'dp', axis=1, tiled=True)  73.6 us
    dot_general x16, matrix products, span_terms(): branch = jnp.dot(hidden, w_down, preferred_element_type=jnp.float32)  63.7 us
    dynamic_update_slice x16, other arithmetic, keep_terms(): lax.dynamic_update_index_in_dim(kept_proj, grad_proj, position, 0)  35.6 us
    all_gather x1, blocking collectives, per_device(): lax.all_gather(down_master.astype(jnp.bfloat16), 'dp', axis=1, tiled=True)  34.7 us
    add x15, other arithmetic, backward(): acc_proj + lax.dynamic_index_in_dim(kept_proj, position, 0, keepdims=False)  34.5 us
  transfers between devices with their start and end apart: 63, of which 17 were waited for; matrix products, arithmetic and copies ran while one was open for 30% of the time, Pallas kernels for 0%

commit v1 on v0

v1 whole, which is shorter than its diff:
```python
import functools

import jax
import jax.numpy as jnp
from jax import lax
from jax.experimental import pallas as pl
from jax.experimental.pallas import tpu as pltpu
from jax.sharding import Mesh, PartitionSpec as P

STEP = 100
AXES = ("x", "zl", "c", "y", "zh")
GROUP = ("x", "zl", "y", "zh")
BF = jnp.bfloat16
F32 = jnp.float32
SLOT = 208
WIN = 256
NT = (((1,), (1,)), ((), ()))
MB = 1024 * 1024


def dot(a, b, dims=(((1,), (0,)), ((), ()))):
    return lax.dot_general(a, b, dims, preferred_element_type=F32)


def iota(shape, dim):
    return lax.broadcasted_iota(jnp.int32, shape, dim)


def adam(master, grad, first_moment, second_moment):
    first_new = 0.9 * first_moment + 0.1 * grad
    second_new = 0.95 * second_moment + 0.05 * grad * grad
    first_hat = first_new / (1.0 - 0.9**STEP)
    second_hat = second_new / (1.0 - 0.95**STEP)
    updated = master - 0.0003 * (first_hat / (jnp.sqrt(second_hat) + 1e-08) + 0.1 * master)
    return (updated, first_new, second_new)


def pack_weights_kernel(proj_ref, down_ref, out_ref):
    d, h = proj_ref.shape[1], proj_ref.shape[2]
    eye = (iota((d, d), 0) == iota((d, d), 1)).astype(BF)
    mats = (
        proj_ref[0].astype(BF),
        proj_ref[1].astype(BF),
        dot(eye, down_ref[...].astype(BF), NT).astype(BF),
    )
    rest = jnp.zeros((d, 128), F32)
    for k, m in enumerate(mats):
        out_ref[:, k * 128 : (k + 1) * 128] = m[:, :128]
        row, col = iota((h, 128), 0), iota((h, 128), 1)
        sel = ((row - 128 == col - 32 * k) & (row >= 128)).astype(BF)
        rest = rest + dot(m, sel)
    out_ref[:, 384:512] = rest.astype(BF)


def pack_weights(proj, down):
    return pl.pallas_call(
        pack_weights_kernel,
        out_shape=jax.ShapeDtypeStruct((proj.shape[1], 512), BF),
        in_specs=[pl.BlockSpec(memory_space=pltpu.VMEM)] * 2,
        out_specs=pl.BlockSpec(memory_space=pltpu.VMEM),
        compiler_params=pltpu.CompilerParams(vmem_limit_bytes=32 * MB),
    )(proj, down)


def pack_tokens_kernel(me_ref, len_ref, own_ref, x_ref, out_ref, start_ref):
    n = len_ref.shape[1]
    rows = x_ref.shape[0]
    me = me_ref[0]
    at = jnp.int32(0)
    for k in range(n):
        start_ref[own_ref[me, k]] = at
        at = at + len_ref[me, k]
    for h in range(n):
        begin = start_ref[h]
        base = pl.multiple_of(jnp.minimum((begin // 16) * 16, rows - WIN), 16)
        sel = (iota((SLOT, WIN), 1) - iota((SLOT, WIN), 0) == begin - base).astype(BF)
        out_ref[h] = dot(sel, x_ref[pl.ds(base, WIN), :]).astype(BF)


def pack_tokens(me, seq_len, seq_owner, x_in):
    n = seq_len.shape[0]
    smem = pl.BlockSpec(memory_space=pltpu.SMEM)
    return pl.pallas_call(
        pack_tokens_kernel,
        out_shape=jax.ShapeDtypeStruct((n, SLOT, x_in.shape[1]), BF),
        in_specs=[smem, smem, smem, pl.BlockSpec(memory_space=pltpu.VMEM)],
        out_specs=pl.BlockSpec(memory_space=pltpu.VMEM),
        scratch_shapes=[pltpu.SMEM((n,), jnp.int32)],
        compiler_params=pltpu.CompilerParams(vmem_limit_bytes=32 * MB),
    )(me, seq_len, seq_owner, x_in)


def unpack_tokens_kernel(me_ref, len_ref, own_ref, slots_ref, out_ref, acc_ref):
    n = len_ref.shape[0]
    rows = out_ref.shape[0]
    me = me_ref[0]
    acc_ref[...] = jnp.zeros_like(acc_ref)
    at = jnp.int32(0)
    for g in range(n):
        count = jnp.int32(0)
        for k in range(n):
            count = count + jnp.where(own_ref[g, k] == me, len_ref[g, k], 0)
        base = pl.multiple_of((at // 16) * 16, 16)
        row, col = iota((WIN, SLOT), 0), iota((WIN, SLOT), 1)
        sel = ((row - col == at - base) & (col < count)).astype(BF)
        acc_ref[pl.ds(base, WIN), :] += dot(sel, slots_ref[g]).astype(BF)
        at = at + count
    out_ref[...] = acc_ref[:rows, :]


def unpack_tokens(me, seq_len, seq_owner, slots, rows):
    smem = pl.BlockSpec(memory_space=pltpu.SMEM)
    d = slots.shape[2]
    return pl.pallas_call(
        unpack_tokens_kernel,
        out_shape=jax.ShapeDtypeStruct((rows, d), BF),
        in_specs=[smem, smem, smem, pl.BlockSpec(memory_space=pltpu.VMEM)],
        out_specs=pl.BlockSpec(memory_space=pltpu.VMEM),
        scratch_shapes=[pltpu.VMEM((rows + WIN, d), BF)],
        compiler_params=pltpu.CompilerParams(vmem_limit_bytes=32 * MB),
    )(me, seq_len, seq_owner, slots)


TB = 256


def layer_kernel(
    tok_a, tok_b, cot_a, cot_b, w_ref, rest_ref, grad_ref, own_ref, part_ref,
    nrm, nrm_t, cot, cot_t, hid, dgate, dup, wg, wu, wd, rest_grad,
):
    step = pl.program_id(0)
    rows, d = tok_a.shape
    total = 2 * rows
    blocks = total // TB

    @pl.when(step == 0)
    def _():
        for half, (t_ref, c_ref) in enumerate(((tok_a, cot_a), (tok_b, cot_b))):
            for i in range(rows // TB):
                at = half * rows + i * TB
                t = t_ref[i * TB : (i + 1) * TB, :].astype(F32)
                scale = lax.rsqrt(jnp.mean(t * t, axis=1, keepdims=True) + 1e-06)
                norm = (t * scale).astype(BF)
                nrm[at : at + TB, :] = norm
                nrm_t[:, at : at + TB] = norm.T
                c = c_ref[i * TB : (i + 1) * TB, :]
                cot[at : at + TB, :] = c
                cot_t[:, at : at + TB] = c.T
        tail = jnp.concatenate([rest_ref[b] for b in range(8)], axis=1)
        row, col = iota((1024, 256), 0), iota((1024, 256), 1)
        for k, dst in enumerate((wg, wu, wd)):
            blk, lane = col // 24, col % 24
            sel = ((row == blk * 128 + 32 * k + lane) & (col < 192)).astype(BF)
            mat = dot(tail, sel).astype(BF)
            if k == 2:
                dst[:, 0:256] = mat
            else:
                dst[...] = mat

    @pl.when(step > 0)
    def _():
        at = pl.multiple_of(step * 256, 256)
        for b in range(2):
            wg[:, b * 128 : (b + 1) * 128] = w_ref[b, :, 0:128]
            wu[:, b * 128 : (b + 1) * 128] = w_ref[b, :, 128:256]
        wd[:, pl.ds(at, 256)] = jnp.concatenate([w_ref[0, :, 256:384], w_ref[1, :, 256:384]], axis=1)

    lanes = pl.ds(pl.multiple_of(step * 256, 256), 256)

    def body(i, _):
        at = pl.ds(pl.multiple_of(i * TB, TB), TB)
        n = nrm[at, :]
        g = dot(n, wg[...])
        u = dot(n, wu[...])
        dh = dot(cot[at, :], wd[:, lanes])
        s = 0.5 * jnp.tanh(0.5 * g) + 0.5
        silu = g * s
        hid[at, lanes] = (silu * u).astype(BF)
        dgate[at, :] = (dh * u * s * (1.0 + g * (1.0 - s))).astype(BF)
        dup[at, :] = (dh * silu).astype(BF)
        return 0

    lax.fori_loop(0, blocks, body, 0)
    g_gate = dot(nrm_t[...], dgate[...]).astype(BF)
    g_up = dot(nrm_t[...], dup[...]).astype(BF)
    g_down = dot(cot_t[...], hid[:, lanes]).astype(BF)

    @pl.when(step == 0)
    def _():
        col, row = iota((256, 1024), 1), iota((256, 1024), 0)
        out = jnp.zeros((d, 1024), F32)
        for k, g in enumerate((g_gate, g_up, g_down)):
            sel = ((col == (row // 24) * 128 + 32 * k + row % 24) & (row < 192)).astype(BF)
            out = out + dot(g, sel)
        rest_grad[...] = out.astype(BF)

    @pl.when(step > 0)
    def _():
        at = pl.multiple_of((step - 1) * 256, 256)
        tail = rest_grad[:, pl.ds(at, 256)]
        for b in range(2):
            half = slice(b * 128, (b + 1) * 128)
            grad_ref[b, :, 0:128] = g_gate[:, half]
            grad_ref[b, :, 128:256] = g_up[:, half]
            grad_ref[b, :, 256:384] = g_down[:, half]
            grad_ref[b, :, 384:512] = tail[:, half]

    @pl.when(step == pl.num_programs(0) - 1)
    def _():
        for i in range(rows // TB):
            at = slice(i * TB, (i + 1) * TB)
            own_ref[at, :] = dot(hid[at, :], wd[...], NT) + tok_a[at, :].astype(F32)
            far = slice(rows + i * TB, rows + (i + 1) * TB)
            part_ref[at, :] = dot(hid[far, :], wd[...], NT).astype(BF)


def layer(tok_a, tok_b, cot_a, cot_b, w):
    rows, d = tok_a.shape
    whole = lambda a: pl.BlockSpec(a.shape, lambda j: (0,) * a.ndim)
    total = 2 * rows
    return pl.pallas_call(
        layer_kernel,
        grid=(5,),
        out_shape=(
            jax.ShapeDtypeStruct((8, d, 512), BF),
            jax.ShapeDtypeStruct((rows, d), F32),
            jax.ShapeDtypeStruct((rows, d), BF),
        ),
        in_specs=[
            whole(tok_a),
            whole(tok_b),
            whole(cot_a),
            whole(cot_b),
            pl.BlockSpec((2, d, 384), lambda j: (jnp.maximum(j - 1, 0), 0, 0)),
            pl.BlockSpec((8, d, 128), lambda j: (0, 0, 3)),
        ],
        out_specs=(
            pl.BlockSpec((2, d, 512), lambda j: (jnp.maximum(j - 1, 0), 0, 0)),
            pl.BlockSpec((rows, d), lambda j: (0, 0)),
            pl.BlockSpec((rows, d), lambda j: (0, 0)),
        ),
        scratch_shapes=[
            pltpu.VMEM((total, d), BF),
            pltpu.VMEM((d, total), BF),
            pltpu.VMEM((total, d), BF),
            pltpu.VMEM((d, total), BF),
            pltpu.VMEM((total, 1280), BF),
            pltpu.VMEM((total, 256), BF),
            pltpu.VMEM((total, 256), BF),
            pltpu.VMEM((d, 256), BF),
            pltpu.VMEM((d, 256), BF),
            pltpu.VMEM((d, 1280), BF),
            pltpu.VMEM((d, 1024), BF),
        ],
        compiler_params=pltpu.CompilerParams(vmem_limit_bytes=60 * MB),
        cost_estimate=pl.CostEstimate(flops=25_000_000_000, bytes_accessed=30_000_000, transcendentals=2_000_000),
    )(tok_a, tok_b, cot_a, cot_b, w, w)


def swap_cores(v):
    return lax.ppermute(v, "c", [(0, 1), (1, 0)])


def per_device(
    x_in, cotangent, seq_len, seq_owner, proj_master, down_master, proj_m, proj_v, down_m, down_v
):
    rows, d = cotangent.shape
    me = (lax.axis_index("y") * lax.axis_size("zh") + lax.axis_index("zh")).reshape(1)
    counts, owners = seq_len[0], seq_owner[0]
    slots = pack_tokens(me, counts, owners, x_in)
    packed = pack_weights(proj_master, down_master)
    slots = lax.all_to_all(slots, ("y", "zh"), 0, 0, tiled=True)
    cot_b = swap_cores(cotangent)
    w = lax.all_to_all(
        jnp.broadcast_to(packed[None], (64,) + packed.shape), GROUP, 0, 0, tiled=True
    )
    tok_a = unpack_tokens(me, counts, owners, slots, rows)
    tok_b = swap_cores(tok_a)
    grads, own, part = layer(tok_a, tok_b, cotangent, cot_b, w.reshape(8, d, 512))
    mixed = (own + swap_cores(part).astype(F32)).astype(BF)
    pieces = lax.all_to_all(grads.reshape(64, d // 8, 512), GROUP, 0, 0, tiled=True)
    total = jnp.sum(pieces.astype(F32), axis=0)
    g_gate = jnp.concatenate([total[:, 0:128], total[:, 384:408]], axis=1)
    g_up = jnp.concatenate([total[:, 128:256], total[:, 416:440]], axis=1)
    g_down = jnp.concatenate([total[:, 256:384], total[:, 448:472]], axis=1).T
    new_proj, new_proj_m, new_proj_v = adam(proj_master, jnp.stack([g_gate, g_up]), proj_m, proj_v)
    new_down, new_down_m, new_down_v = adam(down_master, g_down, down_m, down_v)
    return (mixed, new_proj, new_down, new_proj_m, new_proj_v, new_down_m, new_down_v)


def solution(mesh):
    mesh = Mesh(mesh.devices.reshape(4, 2, 2, 4, 2), AXES)
    blk, dp = ("x", "zl", "c"), ("y", "zh")
    in_specs = (
        P(blk + dp, None),
        P(blk + dp, None),
        P(blk, None, None),
        P(blk, None, None),
        P(None, dp, blk),
        P(blk, dp),
        P(None, dp, blk),
        P(None, dp, blk),
        P(blk, dp),
        P(blk, dp),
    )
    out_specs = (
        P(blk + dp, None),
        P(None, dp, blk),
        P(blk, dp),
        P(None, dp, blk),
        P(None, dp, blk),
        P(blk, dp),
        P(blk, dp),
    )
    return jax.shard_map(
        per_device, mesh=mesh, in_specs=in_specs, out_specs=out_specs, check_vma=False
    )
```

time: 884 us -> 321 us (0.36)
  matrix products: 195 us -> 0 us
  blocking collectives: 108 us -> 0 us
  other arithmetic: 112 us -> 7.31 us
  local copies, waits for them, and re-layouts: 80.7 us -> 11.4 us
  starting transfers between devices: 89.7 us -> 25.8 us
  waiting for transfers between devices: 279 us -> 224 us
  Pallas kernels: 0 us -> 50.3 us
  between operations: 14.3 us -> 0.84 us
    all_to_all x1 -> x3, waiting for transfers between devices: 0.01 us -> 218 us  [the longest x1 89.8 us: per_device(): lax.all_to_all(grads.reshape(64, d // 8, 512), GROUP, 0, 0, tiled=True)]
    dot_general x112 -> x0, matrix products: 195 us -> none  [the longest x16 63.7 us: span_terms(): branch = jnp.dot(hidden, w_down, preferred_element_type=jnp.float32)]
    ppermute x60 -> x3, waiting for transfers between devices: 152 us -> 6.08 us  [swap_cores(): return lax.ppermute(v, 'c', [(0, 1), (1, 0)])]
    unnamed x4 -> x0, waiting for transfers between devices: 127 us -> none
    all_gather x2 -> x0, blocking collectives: 108 us -> none  [the longest x1 73.6 us: per_device(): lax.all_gather(proj_master.astype(jnp.bfloat16), 'dp', axis=1, tiled=True)]
    ppermute x60 -> x3, starting transfers between devices: 81.4 us -> 0.65 us  [swap_cores(): return lax.ppermute(v, 'c', [(0, 1), (1, 0)])]
    add x30 -> x0, other arithmetic: 61.5 us -> none  [the longest x15 34.5 us: backward(): acc_proj + lax.dynamic_index_in_dim(kept_proj, position, 0, keepdims=False)]
    pallas_call x0 -> x4, Pallas kernels: none -> 50.3 us  [the longest x1 46.1 us: layer(): pl.pallas_call(layer_kernel, grid=(5,), out_shape=(jax.ShapeDtypeStruct((...]
  transfers between devices with their start and end apart: 63 -> 6, of which waited for: 17 -> 5; matrix products, arithmetic and copies ran while one was open for 30% -> 1% of each run, Pallas kernels for 0% -> 1%
where the time goes in v1:
time: 321 us; the launch traced here: 320 us
  waiting for transfers between devices  224 us (70%)
  Pallas kernels  50.3 us (16%)
  starting transfers between devices  25.8 us (8%)
  local copies, waits for them, and re-layouts  11.4 us (4%)
  other arithmetic  7.31 us (2%)
    all_to_all x1, waiting for transfers between devices, per_device(): lax.all_to_all(grads.reshape(64, d // 8, 512), GROUP, 0, 0, tiled=True)  89.8 us
    all_to_all x1, waiting for transfers between devices, per_device(): lax.all_to_all(jnp.broadcast_to(packed[None], (64,) + packed.shape), GROU...  86.1 us
    pallas_call x1, Pallas kernels, layer(): pl.pallas_call(layer_kernel, grid=(5,), out_shape=(jax.ShapeDtypeStruct((...  46.1 us
    all_to_all x1, waiting for transfers between devices, per_device(): slots = lax.all_to_all(slots, ('y', 'zh'), 0, 0, tiled=True)  41.9 us
    all_to_all x1, starting transfers between devices, per_device(): lax.all_to_all(grads.reshape(64, d // 8, 512), GROUP, 0, 0, tiled=True)  9.36 us
    all_to_all x1, starting transfers between devices, per_device(): slots = lax.all_to_all(slots, ('y', 'zh'), 0, 0, tiled=True)  8.01 us
    all_to_all x1, starting transfers between devices, per_device(): lax.all_to_all(jnp.broadcast_to(packed[None], (64,) + packed.shape), GROU...  7.79 us
    unnamed x37, local copies, waits for them, and re-layouts  7.39 us
  transfers between devices with their start and end apart: 6, of which 5 were waited for; matrix products, arithmetic and copies ran while one was open for 1% of the time, Pallas kernels for 1%

profile of v1, /device:TPU:0, one launch (start us, length us, event | category | flops | bytes accessed | tf_op | source)
XLA Modules:
  0.0 319.5 jit_solution(6728006184513365595)
XLA Ops:
  0.6 1.8 copy-done.1
  2.4 0.7 copy-done.4
  3.1 0.7 copy-done.6
  3.8 1.7 shard_map.153
  5.6 1.6 copy-done
  7.2 8.0 %all-to-all-start = ((bf16[8,208,896]{2,1,0:T(8,128)(2,1)}), bf16[8,208,896]{2,1,0:T(8,128)(2,1)S(1)}, u32[]{:S(2)}, u32[]{:S(2)}) async-start(bf16[8,208,896]{2,1,0:T(8,128)(2,1)} %copy-done), calls=%async_computation | async-start | bytes 5963776 | tf_op jit(solution)/shard_map/all_to_all | solution.py:272
  15.2 1.0 copy.33.proj_ref
  16.2 0.3 shard_map.155
  16.5 41.9 %all-to-all-done.slots_ref = bf16[8,208,896]{2,1,0:T(8,128)(2,1)S(1)} async-done(((bf16[8,208,896]{2,1,0:T(8,128)(2,1)}), bf16[8,208,896]{2,1,0:T(8,128)(2,1)S(1)}, u32[]{:S(2)}, u32[]{:S(2)}) %all-to-all-start) | async-done | bytes 2981920 | tf_op jit(solution)/shard_map/all_to_all | solution.py:272
  58.4 3.9 %broadcast_in_dim.2 = bf16[64,112,512]{2,1,0:T(8,128)(2,1)} broadcast(bf16[112,512]{1,0:T(8,128)(2,1)S(1)} %shard_map.155), dimensions={1,2} | broadcast | bytes 7454720 | tf_op jit(solution)/shard_map/broadcast_in_dim | solution.py:275
  62.3 7.8 %all-to-all-start.1 = ((bf16[64,112,512]{2,1,0:T(8,128)(2,1)}), bf16[64,112,512]{2,1,0:T(8,128)(2,1)}, u32[]{:S(2)}, u32[]{:S(2)}) async-start(bf16[64,112,512]{2,1,0:T(8,128)(2,1)} %broadcast_in_dim.2), calls=%async_computation.1 | async-start | bytes 14680064 | tf_op jit(solution)/shard_map/all_to_all | solution.py:274
  70.1 0.1 collective-permute-start.1
  70.2 2.1 shard_map.154.tok_a
  72.4 1.1 copy-done.2
  73.5 0.5 collective-permute-start
  73.9 2.8 collective-permute-done.tok_b
  76.7 86.1 %all-to-all-done.1 = bf16[64,112,512]{2,1,0:T(8,128)(2,1)} async-done(((bf16[64,112,512]{2,1,0:T(8,128)(2,1)}), bf16[64,112,512]{2,1,0:T(8,128)(2,1)}, u32[]{:S(2)}, u32[]{:S(2)}) %all-to-all-start.1) | async-done | bytes 7340064 | tf_op jit(solution)/shard_map/all_to_all | solution.py:274
  162.8 46.1 %shard_map.156 = (bf16[8,896,512]{2,1,0:T(8,128)(2,1)}, f32[768,896]{1,0:T(8,128)}, bf16[768,896]{1,0:T(8,128)(2,1)}) custom-call(bf16[768,896]{1,0:T(8,128)(2,1)} %copy-done.2, bf16[768,896]{1,0:T(8,128)(2,1)} %copy-done.14, bf16[768,896]{1,0:T(8,128)(2,1)} %cot_a.1, bf16[768,896]{1,0:T(8,128)(2,1)} %collective-permute-done.1.cot_b, ...), custom_call_target="tpu_custom_call" | custom-call | flops 24999999488 | bytes 30000000 | tf_op jit(solution)/shard_map/pallas_call | solution.py:221
  209.0 9.4 %all-to-all-start.2 = ((bf16[64,112,512]{2,1,0:T(8,128)(2,1)}), bf16[64,112,512]{2,1,0:T(8,128)(2,1)}, u32[]{:S(2)}, u32[]{:S(2)}) async-start(bf16[64,112,512]{2,1,0:T(8,128)(2,1)} %bitcast.21), calls=%async_computation.2 | async-start | bytes 14680064 | tf_op jit(solution)/shard_map/all_to_all | solution.py:281
  218.3 0.1 collective-permute-start.2
  218.4 3.3 %collective-permute-done.2 = bf16[768,896]{1,0:T(8,128)(2,1)S(1)} collective-permute-done((bf16[768,896]{1,0:T(8,128)(2,1)}, bf16[768,896]{1,0:T(8,128)(2,1)S(1)}, u32[]{:S(2)}, u32[]{:S(2)}) %collective-permute-start.2) | collective-permute-done | bytes 1376288 | tf_op jit(solution)/shard_map/ppermute | solution.py:261
  221.7 1.4 add_convert_fusion
  223.2 89.8 %all-to-all-done.2 = bf16[64,112,512]{2,1,0:T(8,128)(2,1)} async-done(((bf16[64,112,512]{2,1,0:T(8,128)(2,1)}), bf16[64,112,512]{2,1,0:T(8,128)(2,1)}, u32[]{:S(2)}, u32[]{:S(2)}) %all-to-all-start.2) | async-done | bytes 7340064 | tf_op jit(solution)/shard_map/all_to_all | solution.py:281
  312.9 4.3 %convert_reduce_fusion = f32[112,512]{1,0:T(8,128)S(1)} fusion(bf16[64,112,512]{2,1,0:T(8,128)(2,1)} %all-to-all-done.2), kind=kLoop, calls=%fused_computation | loop fusion | flops 7282688 | bytes 7569408 | tf_op jit(solution)/shard_map/reduce_sum | solution.py:282
  317.3 0.1 fusion.5
  317.4 0.1 copy.45
  317.4 0.1 copy.44
  317.6 0.1 copy.41
  317.7 0.1 copy.42
  317.8 0.1 copy.40
  318.0 0.7 multiply_subtract_fusion.1
  318.7 0.8 multiply_subtract_fusion
  (29 shorter events, 0.1 us)
Async XLA Ops:
  0.6 1.8 copy-start.1
  2.4 0.7 copy-start.4
  3.1 0.7 copy-start.6
  5.5 1.6 copy-start
  7.1 9.1 %copy-start.3 = (f32[152,112]{1,0:T(8,128)S(1)}, f32[152,112]{1,0:T(8,128)}, u32[]{:S(2)}) copy-start(f32[152,112]{1,0:T(8,128)} %down_ref.1) | copy-start | bytes 204292
  7.2 51.3 %all-to-all-start = ((bf16[8,208,896]{2,1,0:T(8,128)(2,1)}), bf16[8,208,896]{2,1,0:T(8,128)(2,1)S(1)}, u32[]{:S(2)}, u32[]{:S(2)}) async-start(bf16[8,208,896]{2,1,0:T(8,128)(2,1)} %copy-done), calls=%async_computation | async-start | bytes 5963776 | tf_op jit(solution)/shard_map/all_to_all | solution.py:272
  62.3 7.9 %copy-start.5 = (s32[1,8,8]{2,1,0:T(8,128)S(1)}, s32[1,8,8]{2,1,0:T(8,128)}, u32[]{:S(2)}) copy-start(s32[1,8,8]{2,1,0:T(8,128)} %param.12) | copy-start | bytes 772
  62.3 7.9 %copy-start.7 = (s32[1,8,8]{2,1,0:T(8,128)S(1)}, s32[1,8,8]{2,1,0:T(8,128)}, u32[]{:S(2)}) copy-start(s32[1,8,8]{2,1,0:T(8,128)} %param.13) | copy-start | bytes 772
  62.3 100.5 %all-to-all-start.1 = ((bf16[64,112,512]{2,1,0:T(8,128)(2,1)}), bf16[64,112,512]{2,1,0:T(8,128)(2,1)}, u32[]{:S(2)}, u32[]{:S(2)}) async-start(bf16[64,112,512]{2,1,0:T(8,128)(2,1)} %broadcast_in_dim.2), calls=%async_computation.1 | async-start | bytes 14680064 | tf_op jit(solution)/shard_map/all_to_all | solution.py:274
  70.1 3.8 %collective-permute-start.1 = (bf16[768,896]{1,0:T(8,128)(2,1)}, bf16[768,896]{1,0:T(8,128)(2,1)}, u32[]{:S(2)}, u32[]{:S(2)}) collective-permute-start(bf16[768,896]{1,0:T(8,128)(2,1)} %cot_a.1), channel_id=1, source_target_pairs={{0,8},{8,0},{1,9},{9,1},{2,10},{10,2},{3,11},{11,3},{4,12},{12,4},... | collective-permute-start | bytes 4128776 | tf_op jit(solution)/shard_map/ppermute | solution.py:261
  72.4 1.1 copy-start.2
  73.5 3.2 %collective-permute-start = (bf16[768,896]{1,0:T(8,128)(2,1)S(1)}, bf16[768,896]{1,0:T(8,128)(2,1)S(1)}, u32[]{:S(2)}, u32[]{:S(2)}) collective-permute-start(bf16[768,896]{1,0:T(8,128)(2,1)S(1)} %shard_map.154.tok_a), channel_id=1, source_target_pairs={{0,8},{8,0},{1,9},{9,1},{2,10},{10,2},{3,11},{11,3},{4,12},{12,4},... | collective-permute-start | bytes 4128776 | tf_op jit(solution)/shard_map/ppermute | solution.py:261
  76.7 86.1 %copy-start.14 = (bf16[768,896]{1,0:T(8,128)(2,1)}, bf16[768,896]{1,0:T(8,128)(2,1)S(1)}, u32[]{:S(2)}) copy-start(bf16[768,896]{1,0:T(8,128)(2,1)S(1)} %collective-permute-done.tok_b) | copy-start | bytes 4128772
  208.9 12.8 %copy-start.8 = (f32[768,896]{1,0:T(8,128)S(1)}, f32[768,896]{1,0:T(8,128)}, u32[]{:S(2)}) copy-start(f32[768,896]{1,0:T(8,128)} %get-tuple-element.10) | copy-start | bytes 8257540
  209.0 104.0 %all-to-all-start.2 = ((bf16[64,112,512]{2,1,0:T(8,128)(2,1)}), bf16[64,112,512]{2,1,0:T(8,128)(2,1)}, u32[]{:S(2)}, u32[]{:S(2)}) async-start(bf16[64,112,512]{2,1,0:T(8,128)(2,1)} %bitcast.21), calls=%async_computation.2 | async-start | bytes 14680064 | tf_op jit(solution)/shard_map/all_to_all | solution.py:281
  218.3 3.4 %collective-permute-start.2 = (bf16[768,896]{1,0:T(8,128)(2,1)}, bf16[768,896]{1,0:T(8,128)(2,1)S(1)}, u32[]{:S(2)}, u32[]{:S(2)}) collective-permute-start(bf16[768,896]{1,0:T(8,128)(2,1)} %get-tuple-element.11), channel_id=1, source_target_pairs={{0,8},{8,0},{1,9},{9,1},{2,10},{10,2},{3,11},{11,3},{4,12},{12,4},... | collective-permute-start | bytes 4128776 | tf_op jit(solution)/shard_map/ppermute | solution.py:261
  223.1 94.8 %copy-start.12 = (f32[152,112]{1,0:T(8,128)S(1)}, f32[152,112]{1,0:T(8,128)}, u32[]{:S(2)}) copy-start(f32[152,112]{1,0:T(8,128)} %param.18) | copy-start | bytes 204292
  223.1 94.8 %copy-start.13 = (f32[152,112]{1,0:T(8,128)S(1)}, f32[152,112]{1,0:T(8,128)}, u32[]{:S(2)}) copy-start(f32[152,112]{1,0:T(8,128)} %param.19) | copy-start | bytes 204292
  223.1 95.5 %copy-start.9 = (f32[2,112,152]{1,2,0:T(8,128)S(1)}, f32[2,112,152]{1,2,0:T(8,128)}, u32[]{:S(2)}) copy-start(f32[2,112,152]{1,2,0:T(8,128)} %param.14) | copy-start | bytes 408580
  223.1 95.5 %copy-start.10 = (f32[2,112,152]{1,2,0:T(8,128)S(1)}, f32[2,112,152]{1,2,0:T(8,128)}, u32[]{:S(2)}) copy-start(f32[2,112,152]{1,2,0:T(8,128)} %param.16) | copy-start | bytes 408580
  223.1 95.5 %copy-start.11 = (f32[2,112,152]{1,2,0:T(8,128)S(1)}, f32[2,112,152]{1,2,0:T(8,128)}, u32[]{:S(2)}) copy-start(f32[2,112,152]{1,2,0:T(8,128)} %param.17) | copy-start | bytes 408580
